TPU v7x, 32 devices: a whole 2x2x4 slice. The times are simulated.
32 devices in a mesh: groups: 2 (over y), mesh: 8 (over z, x), layer: 2 (over core).
Axes of the slice: x: 2, y: 2, z: 4, core: 2. Of those that a mesh axis runs over, the one named last changes fastest.
Arguments:
- displacement: float32 [3, 16384], P(None, ('groups', 'mesh', 'layer')), parts along dimension 1, may hold values from -6 to 6
- tangent_one: float32 [3, 16384], P(None, ('groups', 'mesh', 'layer')), parts along dimension 1, may hold values from -6 to 6
- tangent_two: float32 [3, 16384], P(None, ('groups', 'mesh', 'layer')), parts along dimension 1, may hold values from -6 to 6
- external_force: float32 [3, 16384], P(None, ('groups', 'mesh', 'layer')), parts along dimension 1, may hold values from -6 to 6
- connectivity: int32 [8, 4096], P(None, ('groups', 'mesh', 'layer')), parts along dimension 1, may hold values from 0 to 543
- element_scale: float32 [4096], P(('groups', 'mesh', 'layer')), parts along dimension 0, may hold values from 0.3 to 3
- halo_nodes: int32 [1024], P(('groups', 'mesh', 'layer')), parts along dimension 0, may hold values from 0 to 511
- slave_nodes: int32 [2048, 128], P(('groups', 'mesh', 'layer')), parts along dimension 0, may hold values from 0 to 512, as said below
- master_nodes: int32 [2048, 128], P(('groups', 'mesh', 'layer')), parts along dimension 0, may hold values from 0 to 512, as said below
- pair_owner: int32 [2048, 1], P(('groups', 'mesh', 'layer')), parts along dimension 0, may hold values from 0 to 15; in each aligned block of 64 rows (0 to 63, 64 to 127, ...) at most 8 rows name the same one
- pair_slot: int32 [2048], P(('groups', 'mesh', 'layer')), parts along dimension 0, may hold values from 0 to 63
- active_flags: int32 [2048, 128], P(('groups', 'mesh', 'layer')), parts along dimension 0, may hold values 0 or 1
- normals: float32 [2048, 3], P(('groups', 'mesh', 'layer')), parts along dimension 0, may hold values from -1 to 1
- initial_gap: float32 [2048, 128], P(('groups', 'mesh', 'layer')), parts along dimension 0, may hold values from -6 to 6
- strain_operator: float32 [48, 24], replicated, may hold values from -1.25 to 1.25
- mortar: float32 [128, 128], replicated
Outputs:
- residual: float32 [3, 16384], P(None, ('groups', 'mesh', 'layer')), parts along dimension 1
- jvp_one: float32 [3, 16384], P(None, ('groups', 'mesh', 'layer')), parts along dimension 1
- jvp_two: float32 [3, 16384], P(None, ('groups', 'mesh', 'layer')), parts along dimension 1
There are 2 independent parts, one for each index of `groups`. A program takes and returns all parts, laid end to end along the dimension named above; an argument that names none is the same for every part. Nothing has to cross between parts.
Inputs may be any that keep to these rules, and one draw needn't show every extreme that they name: `slave_nodes`: each row holds one slave patch's node numbers on its own device, real nodes first, then padding with the value 512; every patch has half of 128 real nodes or more. `master_nodes`: each row holds one master patch's node numbers on its owner device, real nodes first, then padding with the value 512; every patch has half of 128 real nodes or more. `pair_owner`: among the slave patches of one device at most 8 name the same owner, a bound that some block reaches. `halo_nodes`: node numbers of the device that holds the list. `connectivity`: numbers below 512 are the device's own nodes; the others are its ghosts in order.
All inputs are finite; a program needn't handle non-finite values. No bound on the sum of `active_flags` on one device may be relied on, other than what follows from the above.
Results may differ from a plain program's by a relative error of at most 0.00005.
Values sent between devices are 32-bit elements; how exact they have to be, the bound alone decides.
A program may use at most 64 MiB of HBM per device.

v0:
```python
import jax
import jax.numpy as jnp
from jax import lax
from jax.sharding import PartitionSpec as P

PENALTY = 2.0
HIGH = lax.Precision.HIGHEST


def from_behind(value, axis, by):
    length = lax.axis_size(axis)
    return lax.ppermute(value, axis, [(i, (i + by) % length) for i in range(length)])


def strains(extended, corner_matrix, strain_operator):
    rows = extended.shape[0]
    picked = jnp.dot(extended, corner_matrix.T, precision=HIGH).reshape(rows, 8, -1)
    element_values = jnp.transpose(picked, (1, 0, 2)).reshape(24, -1)
    return jnp.dot(strain_operator, element_values, precision=HIGH)


def spread_back(stress, corner_matrix, strain_operator):
    element_force = jnp.dot(strain_operator.T, stress, precision=HIGH).reshape(8, 3, -1)
    element_force = jnp.transpose(element_force, (1, 0, 2)).reshape(3, -1)
    return jnp.dot(element_force, corner_matrix, precision=HIGH)


def on_device(
    displacement,
    tangent_one,
    tangent_two,
    external_force,
    connectivity,
    element_scale,
    halo_nodes,
    slave_nodes,
    master_nodes,
    pair_owner,
    pair_slot,
    active_flags,
    normals,
    initial_gap,
    strain_operator,
    mortar,
):
    node_count = displacement.shape[1]
    extended_width = node_count + halo_nodes.shape[0]
    devices = lax.axis_size(("mesh", "layer"))
    slave_count = slave_nodes.shape[0]
    master_count = master_nodes.shape[0]
    patch_size = slave_nodes.shape[1]
    capacity = max(2, 2 * slave_count // devices)
    corner_matrix = (
        connectivity.reshape(-1)[:, None] == jnp.arange(extended_width, dtype=jnp.int32)[None, :]
    ).astype(jnp.float32)
    owners = pair_owner[:, 0]
    onehot = (owners[:, None] == jnp.arange(devices, dtype=jnp.int32)[None, :]).astype(jnp.int32)
    before = jnp.cumsum(onehot, axis=0) - onehot
    bucket = owners * capacity + jnp.sum(before * onehot, axis=1)
    requests = jnp.full((devices * capacity,), master_count, jnp.int32).at[bucket].set(pair_slot)
    incoming = lax.all_to_all(
        requests.reshape(devices, capacity),
        ("mesh", "layer"),
        split_axis=0,
        concat_axis=0,
        tiled=True,
    ).reshape(-1)
    dummy_patch = jnp.full((1, patch_size), node_count, jnp.int32)
    served_nodes = jnp.concatenate([master_nodes, dummy_patch], axis=0)[incoming]
    live_mask = (slave_nodes < node_count).astype(jnp.float32)
    contact_weight = PENALTY * active_flags.astype(jnp.float32) * live_mask
    normal_rows = normals.T

    def fetch(fields):
        field_count = fields.shape[0]
        flattened = fields.reshape(field_count * 3, node_count)
        ghosts = from_behind(flattened[:, halo_nodes], ("mesh", "layer"), -1)
        extended = jnp.concatenate([flattened, ghosts], axis=1)
        padded = jnp.concatenate([flattened, jnp.zeros((field_count * 3, 1), jnp.float32)], axis=1)
        slave_values = padded[:, slave_nodes].reshape(field_count, 3, slave_count, patch_size)
        slave_normal = jnp.sum(normal_rows[None, :, :, None] * slave_values, axis=1)
        outgoing = padded[:, served_nodes].reshape(field_count * 3, devices, capacity, patch_size)
        received = lax.all_to_all(
            outgoing, ("mesh", "layer"), split_axis=1, concat_axis=1, tiled=True
        )
        master_values = received.reshape(field_count * 3, devices * capacity, patch_size)[:, bucket]
        projected = jnp.dot(
            master_values.reshape(-1, patch_size), mortar.T, precision=HIGH
        ).reshape(field_count, 3, slave_count, patch_size)
        master_normal = jnp.sum(normal_rows[None, :, :, None] * projected, axis=1)
        return (extended.reshape(field_count, 3, extended_width), slave_normal, master_normal)

    def gap_change(slave_normal, master_normal):
        return slave_normal - master_normal

    def finish(internal, multiplier):
        field_count = internal.shape[0]
        internal = internal.reshape(field_count * 3, extended_width)
        returned = from_behind(internal[:, node_count:], ("mesh", "layer"), 1)
        owned = internal[:, :node_count].at[:, halo_nodes].add(returned)
        owned = jnp.concatenate([owned, jnp.zeros((field_count * 3, 1), jnp.float32)], axis=1)
        slave_force = -(normal_rows[None, :, :, None] * multiplier[:, None, :, :]).reshape(
            field_count * 3, slave_count, patch_size
        )
        owned = owned.at[:, slave_nodes].add(slave_force)
        spread = jnp.dot(multiplier.reshape(-1, patch_size), mortar, precision=HIGH).reshape(
            field_count, 1, slave_count, patch_size
        )
        master_force = (normal_rows[None, :, :, None] * spread).reshape(
            field_count * 3, slave_count, patch_size
        )
        outgoing = (
            jnp.zeros((field_count * 3, devices * capacity, patch_size), jnp.float32)
            .at[:, bucket]
            .set(master_force)
        )
        received = lax.all_to_all(
            outgoing.reshape(field_count * 3, devices, capacity, patch_size),
            ("mesh", "layer"),
            split_axis=1,
            concat_axis=1,
            tiled=True,
        )
        received = received.reshape(field_count * 3, devices * capacity, patch_size)
        owned = owned.at[:, served_nodes].add(received)
        return owned[:, :node_count].reshape(field_count, 3, node_count)

    extended, slave_normal, master_normal = fetch(displacement[None])
    base_extended = extended[0]
    base_slave_normal = slave_normal[0]
    base_master_normal = master_normal[0]
    strain = strains(base_extended, corner_matrix, strain_operator)
    hyperbolic = jnp.tanh(strain)
    stress = element_scale * (strain + 0.5 * hyperbolic)
    stiffness = element_scale * (1.0 + 0.5 * (1.0 - hyperbolic * hyperbolic))
    internal = spread_back(stress, corner_matrix, strain_operator)
    gap_now = initial_gap + gap_change(base_slave_normal, base_master_normal)
    multiplier = contact_weight * jax.nn.softplus(-gap_now)
    contact_slope = -contact_weight * jax.nn.sigmoid(-gap_now)
    internal, multiplier, stiffness, contact_slope = (
        internal,
        multiplier,
        stiffness,
        contact_slope,
    )
    residual = finish(internal[None], multiplier[None])[0] - external_force
    products = []
    for vector in (tangent_one, tangent_two):
        extended, slave_normal, master_normal = fetch(vector[None])
        tangent_extended = extended[0]
        tangent_slave_normal = slave_normal[0]
        tangent_master_normal = master_normal[0]
        tangent_strain = strains(tangent_extended, corner_matrix, strain_operator)
        tangent_internal = spread_back(stiffness * tangent_strain, corner_matrix, strain_operator)
        tangent_multiplier = contact_slope * gap_change(tangent_slave_normal, tangent_master_normal)
        internal = tangent_internal
        multiplier = tangent_multiplier
        products.append(finish(internal[None], multiplier[None])[0])
    jvp_one = products[0]
    jvp_two = products[1]
    return (residual, jvp_one, jvp_two)


def solution(mesh):
    return jax.shard_map(
        on_device,
        mesh=mesh,
        in_specs=(
            P(None, ("groups", "mesh", "layer")),
            P(None, ("groups", "mesh", "layer")),
            P(None, ("groups", "mesh", "layer")),
            P(None, ("groups", "mesh", "layer")),
            P(None, ("groups", "mesh", "layer")),
            P(("groups", "mesh", "layer")),
            P(("groups", "mesh", "layer")),
            P(("groups", "mesh", "layer"), None),
            P(("groups", "mesh", "layer"), None),
            P(("groups", "mesh", "layer"), None),
            P(("groups", "mesh", "layer")),
            P(("groups", "mesh", "layer"), None),
            P(("groups", "mesh", "layer"), None),
            P(("groups", "mesh", "layer"), None),
            P(),
            P(),
        ),
        out_specs=(
            P(None, ("groups", "mesh", "layer")),
            P(None, ("groups", "mesh", "layer")),
            P(None, ("groups", "mesh", "layer")),
        ),
        check_vma=False,
    )
```

profile of v0, /device:TPU:1, one launch (start us, length us, event | category | flops | bytes accessed | tf_op | source)
XLA Modules:
  0.0 856.2 jit_solution(9105599786025931332)
XLA Ops:
  6.8 8.7 %all-to-all-start = ((s32[16,1,8]{2,1,0:T(1,128)}), s32[16,1,8]{2,1,0:T(1,128)S(1)}, u32[]{:S(2)}, u32[]{:S(2)}) async-start(s32[16,1,8]{2,1,0:T(1,128)} %bitcast.16), calls=%async_computation | async-start | bytes 16384 | tf_op jit(solution)/shard_map/all_to_all | solution.py:61
  24.6 27.7 %gather_fusion.10 = f32[8192,3]{1,0:T(8,128)} fusion(f32[3,513]{0,1:T(8,128)S(1)} %concatenate.39, s32[8192]{0:T(1024)S(1)} %broadcast_clamp_fusion.1), kind=kCustom, calls=%fused_computation.10 | custom fusion | bytes 229376 | tf_op jit(solution)/shard_map/gather | solution.py:80
  55.1 27.7 %gather_fusion.6 = f32[8192,3]{1,0:T(8,128)} fusion(f32[3,513]{0,1:T(8,128)S(1)} %concatenate.36, s32[8192]{0:T(1024)S(1)} %broadcast_clamp_fusion.1), kind=kCustom, calls=%fused_computation.6 | custom fusion | bytes 229376 | tf_op jit(solution)/shard_map/gather | solution.py:80
  85.8 27.7 %gather_fusion.1 = f32[8192,3]{1,0:T(8,128)} fusion(f32[3,513]{0,1:T(8,128)S(1)} %concatenate.32, s32[8192]{0:T(1024)S(1)} %broadcast_clamp_fusion.1), kind=kCustom, calls=%fused_computation.1 | custom fusion | bytes 229376 | tf_op jit(solution)/shard_map/gather | solution.py:80
  120.3 54.4 %gather_fusion.11 = f32[16384,3]{1,0:T(8,128)} fusion(f32[3,513]{0,1:T(8,128)S(1)} %concatenate.39, s32[16384]{0:T(1024)S(1)} %broadcast_clamp_fusion), kind=kCustom, calls=%fused_computation.11 | custom fusion | bytes 458752 | tf_op jit(solution)/shard_map/gather | solution.py:82
  174.7 5.9 copy.173
  186.1 54.4 %gather_fusion.3 = f32[16384,3]{1,0:T(8,128)} fusion(f32[3,513]{0,1:T(8,128)S(1)} %concatenate.32, s32[16384]{0:T(1024)S(1)} %broadcast_clamp_fusion), kind=kCustom, calls=%fused_computation.3 | custom fusion | bytes 458752 | tf_op jit(solution)/shard_map/gather | solution.py:82
  240.6 5.8 copy.140
  246.4 6.1 all-to-all-start.1
  253.6 54.4 %gather_fusion.7 = f32[16384,3]{1,0:T(8,128)} fusion(f32[3,513]{0,1:T(8,128)S(1)} %concatenate.36, s32[16384]{0:T(1024)S(1)} %broadcast_clamp_fusion), kind=kCustom, calls=%fused_computation.7 | custom fusion | bytes 458752 | tf_op jit(solution)/shard_map/gather | solution.py:82
  308.1 5.9 copy.157
  314.7 6.0 all-to-all-start.3
  322.5 6.5 all-to-all-done.3
  345.7 4.5 all-to-all-start.4
  360.6 7.8 all-to-all-start.6
  376.3 46.3 %scatter_fusion.1 = f32[3,513]{0,1:T(8,128)S(1)} fusion(f32[3,513]{0,1:T(8,128)S(1)} %concatenate.31, s32[8192]{0:T(1024)S(1)} %fusion.30, f32[8192,3]{1,0:T(8,128)} %bitcast.177), kind=kCustom, calls=%fused_computation.15 | custom fusion | flops 24576 | bytes 327680 | tf_op jit(solution)/shard_map/scatter-add | solution.py:105
  422.6 46.3 %scatter_fusion.5 = f32[3,513]{0,1:T(8,128)S(1)} fusion(f32[3,513]{0,1:T(8,128)S(1)} %concatenate.35, s32[8192]{0:T(1024)S(1)} %fusion.30, f32[8192,3]{1,0:T(8,128)} %bitcast.176), kind=kCustom, calls=%fused_computation.19 | custom fusion | flops 24576 | bytes 327680 | tf_op jit(solution)/shard_map/scatter-add | solution.py:105
  468.9 46.3 %scatter_fusion.9 = f32[3,513]{0,1:T(8,128)S(1)} fusion(f32[3,513]{0,1:T(8,128)S(1)} %concatenate.38, s32[8192]{0:T(1024)S(1)} %fusion.30, f32[8192,3]{1,0:T(8,128)} %bitcast.175), kind=kCustom, calls=%fused_computation.23 | custom fusion | flops 24576 | bytes 327680 | tf_op jit(solution)/shard_map/scatter-add | solution.py:105
  515.3 4.6 copy.187
  519.9 108.4 %scatter_fusion.3 = f32[3,513]{0,1:T(8,128)S(1)} fusion(f32[3,513]{0,1:T(8,128)S(1)} %scatter_fusion.1, s32[16384]{0:T(1024)S(1)} %fusion.26, f32[16384,3]{1,0:T(8,128)} %bitcast.171), kind=kCustom, calls=%fused_computation.17 | custom fusion | flops 49152 | bytes 655360 | tf_op jit(solution)/shard_map/scatter-add | solution.py:125
  629.1 4.6 copy.191
  633.7 108.1 %scatter_fusion.7 = f32[3,513]{0,1:T(8,128)S(1)} fusion(f32[3,513]{0,1:T(8,128)S(1)} %scatter_fusion.5, s32[16384]{0:T(1024)S(1)} %fusion.26, f32[16384,3]{1,0:T(8,128)} %bitcast.172), kind=kCustom, calls=%fused_computation.21 | custom fusion | flops 49152 | bytes 655360 | tf_op jit(solution)/shard_map/scatter-add | solution.py:125
  742.6 4.6 copy.195
  747.3 108.1 %scatter_fusion.11 = f32[3,513]{0,1:T(8,128)S(1)} fusion(f32[3,513]{0,1:T(8,128)S(1)} %scatter_fusion.9, s32[16384]{0:T(1024)S(1)} %fusion.26, f32[16384,3]{1,0:T(8,128)} %bitcast.169), kind=kCustom, calls=%fused_computation.25 | custom fusion | flops 49152 | bytes 655360 | tf_op jit(solution)/shard_map/scatter-add | solution.py:125
  (160 shorter events, 73.7 us)
Async XLA Ops:
  0.6 320.8 %copy-start = (f32[128,128]{1,0:T(8,128)S(1)}, f32[128,128]{1,0:T(8,128)}, u32[]{:S(2)}) copy-start(f32[128,128]{1,0:T(8,128)} %param.31) | copy-start | bytes 196612
  2.8 113.9 %collective-permute-start = (f32[3,32]{0,1:T(8,128)S(1)}, f32[3,32]{0,1:T(8,128)S(1)}, u32[]{:S(2)}, u32[]{:S(2)}) collective-permute-start(f32[3,32]{0,1:T(8,128)S(1)} %bitcast.205), channel_id=1, source_target_pairs={{0,15},{1,0},{2,1},{3,2},{4,3},{5,4},{6,5},{7,6},{8,7},{9,8},{10,9... | collective-permute-start | bytes 1160 | tf_op jit(solution)/shard_map/ppermute | solution.py:12
  6.8 111.5 %all-to-all-start = ((s32[16,1,8]{2,1,0:T(1,128)}), s32[16,1,8]{2,1,0:T(1,128)S(1)}, u32[]{:S(2)}, u32[]{:S(2)}) async-start(s32[16,1,8]{2,1,0:T(1,128)} %bitcast.16), calls=%async_computation | async-start | bytes 16384 | tf_op jit(solution)/shard_map/all_to_all | solution.py:61
  16.9 167.6 %collective-permute-start.2 = (f32[3,32]{0,1:T(8,128)S(1)}, f32[3,32]{0,1:T(8,128)S(1)}, u32[]{:S(2)}, u32[]{:S(2)}) collective-permute-start(f32[3,32]{0,1:T(8,128)S(1)} %bitcast.204), channel_id=1, source_target_pairs={{0,15},{1,0},{2,1},{3,2},{4,3},{5,4},{6,5},{7,6},{8,7},{9,8},{10,9... | collective-permute-start | bytes 1160 | tf_op jit(solution)/shard_map/ppermute | solution.py:12
  18.6 322.0 %collective-permute-start.4 = (f32[3,32]{0,1:T(8,128)S(1)}, f32[3,32]{0,1:T(8,128)S(1)}, u32[]{:S(2)}, u32[]{:S(2)}) collective-permute-start(f32[3,32]{0,1:T(8,128)S(1)} %bitcast.203), channel_id=1, source_target_pairs={{0,15},{1,0},{2,1},{3,2},{4,3},{5,4},{6,5},{7,6},{8,7},{9,8},{10,9... | collective-permute-start | bytes 1160 | tf_op jit(solution)/shard_map/ppermute | solution.py:12
  82.8 33.5 %copy-start.4 = (f32[64,3]{0,1:T(4,128)S(1)}, f32[64,3]{0,1:T(4,128)}, u32[]{:S(2)}) copy-start(f32[64,3]{0,1:T(4,128)} %param.28) | copy-start | bytes 2308
  82.8 33.6 %copy-start.8 = (f32[3,512]{1,0:T(4,128)S(1)}, f32[3,512]{1,0:T(4,128)}, u32[]{:S(2)}) copy-start(f32[3,512]{1,0:T(4,128)} %param.19) | copy-start | bytes 18436
  85.7 30.9 %copy-start.7 = (s32[64,128]{1,0:T(8,128)S(1)}, s32[64,128]{1,0:T(8,128)}, u32[]{:S(2)}) copy-start(s32[64,128]{1,0:T(8,128)} %param.24) | copy-start | bytes 98308
  85.7 31.0 %copy-start.9 = (f32[3,512]{1,0:T(4,128)S(1)}, f32[3,512]{1,0:T(4,128)}, u32[]{:S(2)}) copy-start(f32[3,512]{1,0:T(4,128)} %param.16) | copy-start | bytes 18436
  85.7 31.0 %copy-start.13 = (s32[8,128]{1,0:T(8,128)S(1)}, s32[8,128]{1,0:T(8,128)}, u32[]{:S(2)}) copy-start(s32[8,128]{1,0:T(8,128)} %param.20) | copy-start | bytes 12292
  85.7 32.3 %copy-start.2 = (f32[48,24]{0,1:T(8,128)S(1)}, f32[48,24]{0,1:T(8,128)}, u32[]{:S(2)}) copy-start(f32[48,24]{0,1:T(8,128)} %param.30) | copy-start | bytes 13828
  180.6 65.8 %all-to-all-start.5 = ((f32[3,16,8,128]{3,2,0,1:T(8,128)}), f32[3,16,8,128]{3,2,0,1:T(8,128)S(1)}, u32[]{:S(2)}, u32[]{:S(2)}) async-start(f32[3,16,8,128]{3,2,0,1:T(8,128)} %copy.173), calls=%async_computation.5 | async-start | bytes 393216 | tf_op jit(solution)/shard_map/all_to_all | solution.py:83
  246.4 68.3 %all-to-all-start.1 = ((f32[3,16,8,128]{3,2,0,1:T(8,128)}), f32[3,16,8,128]{3,2,0,1:T(8,128)S(1)}, u32[]{:S(2)}, u32[]{:S(2)}) async-start(f32[3,16,8,128]{3,2,0,1:T(8,128)} %copy.140), calls=%async_computation.1 | async-start | bytes 393216 | tf_op jit(solution)/shard_map/all_to_all | solution.py:83
  308.1 14.0 %copy-start.5 = (f32[64,128]{1,0:T(8,128)S(1)}, f32[64,128]{1,0:T(8,128)}, u32[]{:S(2)}) copy-start(f32[64,128]{1,0:T(8,128)} %param.29) | copy-start | bytes 98308
  308.1 14.0 %copy-start.6 = (s32[64,128]{1,0:T(8,128)S(1)}, s32[64,128]{1,0:T(8,128)}, u32[]{:S(2)}) copy-start(s32[64,128]{1,0:T(8,128)} %param.27) | copy-start | bytes 98308
  313.9 26.7 %copy-start.11 = (f32[3,512]{1,0:T(4,128)S(1)}, f32[3,512]{1,0:T(4,128)}, u32[]{:S(2)}) copy-start(f32[3,512]{1,0:T(4,128)} %param.18) | copy-start | bytes 18436
  314.7 14.3 %all-to-all-start.3 = ((f32[3,16,8,128]{3,2,0,1:T(8,128)}), f32[3,16,8,128]{3,2,0,1:T(8,128)S(1)}, u32[]{:S(2)}, u32[]{:S(2)}) async-start(f32[3,16,8,128]{3,2,0,1:T(8,128)} %copy.157), calls=%async_computation.3 | async-start | bytes 393216 | tf_op jit(solution)/shard_map/all_to_all | solution.py:83
  333.6 12.1 %all-to-all-start.2 = ((f32[3,16,8,128]{3,2,0,1:T(8,128)}), f32[3,16,8,128]{3,2,0,1:T(8,128)S(1)}, u32[]{:S(2)}, u32[]{:S(2)}) async-start(f32[3,16,8,128]{3,2,0,1:T(8,128)} %copy.145), calls=%async_computation.2 | async-start | bytes 393216 | tf_op jit(solution)/shard_map/all_to_all | solution.py:117
  338.7 15.0 %collective-permute-start.1 = (f32[3,32]{1,0:T(4,128)S(1)}, f32[3,32]{1,0:T(4,128)S(1)}, u32[]{:S(2)}, u32[]{:S(2)}) collective-permute-start(f32[3,32]{1,0:T(4,128)S(1)} %slice.63), channel_id=1, source_target_pairs={{0,1},{1,2},{2,3},{3,4},{4,5},{5,6},{6,7},{7,8},{8,9},{9,10},{10,1... | collective-permute-start | bytes 1160 | tf_op jit(solution)/shard_map/ppermute | solution.py:12
  345.7 14.9 %all-to-all-start.4 = ((f32[3,16,8,128]{3,2,0,1:T(8,128)}), f32[3,16,8,128]{3,2,0,1:T(8,128)S(1)}, u32[]{:S(2)}, u32[]{:S(2)}) async-start(f32[3,16,8,128]{3,2,0,1:T(8,128)} %copy.162), calls=%async_computation.4 | async-start | bytes 393216 | tf_op jit(solution)/shard_map/all_to_all | solution.py:117
  351.4 2.4 collective-permute-start.3
  353.4 1.2 collective-permute-start.5
  360.6 382.0 %all-to-all-start.6 = ((f32[3,16,8,128]{3,2,0,1:T(8,128)}), f32[3,16,8,128]{3,2,0,1:T(8,128)S(1)}, u32[]{:S(2)}, u32[]{:S(2)}) async-start(f32[3,16,8,128]{3,2,0,1:T(8,128)} %copy.178), calls=%async_computation.6 | async-start | bytes 393216 | tf_op jit(solution)/shard_map/all_to_all | solution.py:117
  742.6 113.6 %copy-start.1 = (f32[128,128]{1,0:T(8,128)S(1)}, f32[128,128]{1,0:T(8,128)}, u32[]{:S(2)}) copy-start(f32[128,128]{1,0:T(8,128)} %param.31) | copy-start | bytes 196612
  (3 other events, 33.3 us)
where the time goes:
time: 859 us; the launch traced here: 856 us
  other arithmetic  472 us (55%)
  local copies, waits for them, and re-layouts  317 us (37%)
  starting transfers between devices  49.4 us (6%)
  matrix products  9.32 us (1%)
    scatter-add x3, other arithmetic, finish(): owned = owned.at[:, served_nodes].add(received)  325 us
    gather x3, local copies, waits for them, and re-layouts, fetch(): padded[:, served_nodes]  163 us
    scatter-add x3, other arithmetic, finish(): owned = owned.at[:, slave_nodes].add(slave_force)  139 us
    gather x6, local copies, waits for them, and re-layouts, fetch(): padded[:, slave_nodes].reshape(field_count, 3, slave_count, patch_size)  91.7 us
    reshape x3, local copies, waits for them, and re-layouts, fetch(): padded[:, served_nodes]  17.6 us
  transfers between devices with their start and end apart: 13, of which 3 were waited for; matrix products, arithmetic and copies ran while one was open for 80% of the time, Pallas kernels for 0%

commit v1 on v0

v1 whole, which is shorter than its diff:
```python
import functools

import jax
import jax.numpy as jnp
from jax import lax
from jax.experimental import pallas as pl
from jax.experimental.pallas import tpu as pltpu
from jax.sharding import PartitionSpec as P

PENALTY = 2.0
HIGH = lax.Precision.HIGHEST
LANES = 128
ROWS = 16
FIELDS = 3
NN = ((1,), (0,))
NT = ((1,), (1,))
TN = ((0,), (0,))
F32 = jnp.float32
BF16 = jnp.bfloat16


def dot(left, right, dims):
    return lax.dot_general(
        left, right, (dims, ((), ())), precision=HIGH, preferred_element_type=F32
    )


def dot16(left, right, dims):
    return lax.dot_general(left, right, (dims, ((), ())), preferred_element_type=F32)


def halves(value):
    top = value.astype(BF16)
    return top, (value - top.astype(F32)).astype(BF16)


def thirds(value):
    top = value.astype(BF16)
    rest = value - top.astype(F32)
    middle = rest.astype(BF16)
    return top, middle, (rest - middle.astype(F32)).astype(BF16)


def iota(shape, dim):
    return lax.broadcasted_iota(jnp.int32, shape, dim)


def where01(mask):
    return jnp.where(mask, 1.0, 0.0).astype(F32)


def column(index, by=LANES):
    return slice(index * by, (index + 1) * by)


def lookup(tile_of, tiles, index):
    lane = jnp.bitwise_and(index, LANES - 1)
    tile = jnp.right_shift(index, 7)
    found = jnp.zeros(index.shape, F32)
    for number in range(tiles):
        table = jnp.broadcast_to(tile_of(number), index.shape)
        picked = jnp.take_along_axis(table, lane, axis=1, mode="promise_in_bounds")
        found = jnp.where(tile == number, picked, found)
    return found


def add_operands(values, index, tiles):
    lane = jnp.bitwise_and(index, LANES - 1)
    tile = jnp.right_shift(index, 7)
    top = values.astype(BF16).astype(F32)
    both = jnp.concatenate([top, values - top], axis=0)
    left = jnp.concatenate(
        [jnp.where(tile == number, both, 0.0).astype(BF16) for number in range(tiles)], axis=0
    )
    right = where01(lane == iota((LANES, LANES), 0)).astype(BF16)
    return left, right


def add_rows(value_ref, index_ref, first, groups, tiles, total):
    def step(group, total):
        rows = index_ref[pl.ds(pl.multiple_of(group * 8, 8), 8), :]
        pairs = [
            add_operands(value_ref[first + group * 8 + k], rows[k : k + 1, :], tiles)
            for k in range(8)
        ]
        left = jnp.concatenate([pair[0] for pair in pairs], axis=1)
        right = jnp.concatenate([pair[1] for pair in pairs], axis=1)
        return total + dot16(left, right, NT)

    return lax.fori_loop(0, groups, step, total)


def tile_sum(total, number):
    start = number * 2 * ROWS
    return total[start : start + ROWS] + total[start + ROWS : start + 2 * ROWS]


def kernel(
    devices,
    layers,
    share,
    displacement,
    tangent_one,
    tangent_two,
    external_force,
    connectivity,
    element_scale,
    halo_nodes,
    slave_nodes,
    master_nodes,
    pair_owner,
    pair_slot,
    active_flags,
    normals,
    initial_gap,
    strain_operator,
    mortar,
    residual,
    jvp_one,
    jvp_two,
    field,
    halo_send,
    halo_recv,
    ghost_send,
    ghost_recv,
    request_send,
    request_recv,
    master_send,
    master_recv,
    force_send,
    force_recv,
    slave_values,
    element_values,
    master_values,
    send_sem,
    recv_sem,
    near_send_sem,
    near_recv_sem,
):
    node_count = displacement.shape[1]
    node_tiles = node_count // LANES
    slaves = slave_nodes.shape[0]
    masters = master_nodes.shape[0]
    buckets = devices * share
    group = lax.axis_index("groups")
    me = lax.axis_index("mesh") * layers + lax.axis_index("layer")

    def device(peer):
        return (group, peer // layers, lax.rem(peer, layers))

    def block(ref, peer):
        return ref.at[pl.ds(pl.multiple_of(peer * share, share), share), :]

    def far_copy(source, target, phase, k, peer, slot):
        return pltpu.make_async_remote_copy(
            src_ref=block(source, peer),
            dst_ref=block(target, slot),
            send_sem=send_sem.at[phase, k],
            recv_sem=recv_sem.at[phase, k],
            device_id=device(peer),
            device_id_type=pl.DeviceIdType.MESH,
        )

    def send(source, target, phase):
        def one(k, carry):
            far_copy(source, target, phase, k, lax.rem(me + k, devices), me).start()
            return carry

        lax.fori_loop(1, devices, one, 0)
        mine = pl.ds(pl.multiple_of(me * share, share), share)
        target[mine, :] = source[mine, :]

    def receive(source, target, phase):
        def one(k, carry):
            behind = lax.rem(me + devices - k, devices)
            far_copy(source, target, phase, k, lax.rem(me + k, devices), behind).wait_recv()
            return carry

        lax.fori_loop(1, devices, one, 0)

    def sent(source, target, phase):
        def one(k, carry):
            far_copy(source, target, phase, k, lax.rem(me + k, devices), me).wait_send()
            return carry

        lax.fori_loop(1, devices, one, 0)

    def near_copy(source, target, number, peer):
        return pltpu.make_async_remote_copy(
            src_ref=source,
            dst_ref=target,
            send_sem=near_send_sem.at[number],
            recv_sem=near_recv_sem.at[number],
            device_id=device(peer),
            device_id_type=pl.DeviceIdType.MESH,
        )

    after = lax.rem(me + 1, devices)
    before = lax.rem(me + devices - 1, devices)

    barrier = pltpu.get_barrier_semaphore()

    def greet(k, carry):
        pl.semaphore_signal(
            barrier,
            inc=1,
            device_id=device(lax.rem(me + k, devices)),
            device_id_type=pl.DeviceIdType.MESH,
        )
        return carry

    lax.fori_loop(1, devices, greet, 0)

    owner_column = pair_owner[...].astype(F32)
    first = iota((slaves, slaves), 0)
    second = iota((slaves, slaves), 1)
    owner_row = jnp.sum(jnp.where(first == second, owner_column, 0.0), axis=0, keepdims=True)
    slot_column = jnp.sum(
        jnp.where(first == second, pair_slot[...].astype(F32), 0.0), axis=1, keepdims=True
    )
    same = where01(owner_column == owner_row)
    rank_row = jnp.sum(jnp.where(first < second, same, 0.0), axis=0, keepdims=True)
    rank_column = jnp.sum(jnp.where(second < first, same, 0.0), axis=1, keepdims=True)
    bucket_row = owner_row * share + rank_row
    bucket_column = owner_column * share + rank_column
    to_bucket = where01(iota((buckets, slaves), 0).astype(F32) == bucket_row)
    normal = normals[...]
    lane = iota((slaves, LANES), 1)
    wanted = jnp.where(lane == 0, slot_column, 0.0)
    for c in range(3):
        wanted = jnp.where(lane == c + 1, normal[:, c : c + 1], wanted)
    request_send[...] = dot(to_bucket, wanted, NN)

    field[...] = jnp.zeros(field.shape, F32)
    for f, source in enumerate((displacement, tangent_one, tangent_two)):
        field[3 * f : 3 * f + 3, 0:node_count] = source[...]
    ghosts = halo_nodes.shape[1]
    halo_row = jnp.concatenate(
        [halo_nodes[...], jnp.full((1, LANES - ghosts), node_count, jnp.int32)], axis=1
    )
    halo_send[...] = lookup(
        lambda number: field[:, column(number)],
        node_tiles,
        jnp.broadcast_to(halo_row, (ROWS, LANES)),
    )

    pl.semaphore_wait(barrier, devices - 1)
    send(request_send, request_recv, 0)
    near_copy(halo_send, halo_recv, 0, before).start()

    def nodal(index, fc):
        return lookup(lambda number: field[fc : fc + 1, column(number)], node_tiles, index)

    master_index = master_nodes[...]
    parts = [thirds(nodal(master_index, fc)) for fc in range(9)]
    served = jnp.concatenate(
        [jnp.concatenate([part[k] for part in parts], axis=1) for k in range(3)], axis=0
    )
    receive(request_send, request_recv, 0)
    request = request_recv[...]
    slot = request[:, 0:1]
    pick = where01(
        lax.rem(iota((buckets, 3 * masters), 1), masters).astype(F32) == slot
    ).astype(BF16)
    chosen = dot16(pick, served, NN)
    for f in range(FIELDS):
        value = request[:, 1:2] * chosen[:, column(3 * f)]
        for c in range(1, 3):
            value = value + request[:, c + 1 : c + 2] * chosen[:, column(3 * f + c)]
        master_send[:, column(f)] = value
    send(master_send, master_recv, 1)

    slave_index = slave_nodes[...]
    slave_normal = []
    for f in range(FIELDS):
        value = normal[:, 0:1] * nodal(slave_index, 3 * f)
        for c in range(1, 3):
            value = value + normal[:, c : c + 1] * nodal(slave_index, 3 * f + c)
        slave_normal.append(value)
    live = jnp.where(slave_index < node_count, PENALTY, 0.0)
    weight = active_flags[...].astype(F32) * live

    near_copy(halo_send, halo_recv, 0, before).wait_recv()
    field[:, node_count : node_count + LANES] = halo_recv[...]
    corner = connectivity[...]
    elements = jnp.concatenate(
        [
            jnp.concatenate(
                [
                    lookup(
                        lambda number: field[3 * f + c : 3 * f + c + 1, column(number)],
                        node_tiles + 1,
                        corner,
                    )
                    for c in range(3)
                ],
                axis=0,
            )
            for f in range(FIELDS)
        ],
        axis=1,
    )
    entries = strain_operator.shape[1]
    order = iota((entries, entries), 1)
    operator = dot(
        strain_operator[...],
        where01(iota((entries, entries), 0) == 3 * lax.rem(order, 8) + order // 8),
        NN,
    )
    strain = dot(operator, elements, NN)
    scale = element_scale[...]
    base = strain[:, 0:LANES]
    hyperbolic = jnp.tanh(base)
    stiffness = scale * (1.0 + 0.5 * (1.0 - hyperbolic * hyperbolic))
    stress = jnp.concatenate(
        [
            scale * (base + 0.5 * hyperbolic),
            stiffness * strain[:, column(1)],
            stiffness * strain[:, column(2)],
        ],
        axis=1,
    )
    element_force = dot(operator, stress, TN)
    element_values[...] = jnp.zeros(element_values.shape, F32)
    for f in range(FIELDS):
        for c in range(3):
            element_values[:, 3 * f + c, :] = element_force[8 * c : 8 * c + 8, column(f)]
    total = jnp.zeros((2 * ROWS * (node_tiles + 1), LANES), F32)
    total = add_rows(element_values, connectivity, 0, 1, node_tiles + 1, total)
    ghost_send[...] = tile_sum(total, node_tiles)
    near_copy(ghost_send, ghost_recv, 1, after).start()
    total = total[: 2 * ROWS * node_tiles]

    receive(master_send, master_recv, 1)
    from_bucket = where01(iota((slaves, buckets), 1).astype(F32) == bucket_column).astype(BF16)
    top, rest = halves(master_recv[...])
    fetched = dot16(from_bucket, top, NN) + dot16(from_bucket, rest, NN)
    fetched = jnp.concatenate([fetched[:, column(f)] for f in range(FIELDS)], axis=0)
    projected = dot(fetched, mortar[...], NT)
    change = [slave_normal[f] - projected[column(f, slaves)] for f in range(FIELDS)]
    closing = -(initial_gap[...] + change[0])
    small = jnp.exp(-jnp.abs(closing))
    slope = -weight * jnp.where(closing >= 0.0, 1.0, small) / (1.0 + small)
    multiplier = [
        weight * (jnp.maximum(closing, 0.0) + jnp.log1p(small)),
        slope * change[1],
        slope * change[2],
    ]
    spread = dot(jnp.concatenate(multiplier, axis=0), mortar[...], NN)
    spread = jnp.concatenate([spread[column(f, slaves)] for f in range(FIELDS)], axis=1)
    top, rest = halves(spread)
    to_bucket = to_bucket.astype(BF16)
    force_send[...] = dot16(to_bucket, top, NN) + dot16(to_bucket, rest, NN)
    send(force_send, force_recv, 2)

    slave_values[...] = jnp.zeros(slave_values.shape, F32)
    for f in range(FIELDS):
        for c in range(3):
            slave_values[:, 3 * f + c, :] = -normal[:, c : c + 1] * multiplier[f]
    total = add_rows(slave_values, slave_nodes, 0, slaves // 8, node_tiles, total)

    near_copy(ghost_send, ghost_recv, 1, after).wait_recv()
    left, right = add_operands(ghost_recv[...], halo_row, node_tiles)
    total = total + dot16(left, right, NT)

    master_values[...] = jnp.zeros(master_values.shape, F32)
    at_slot = jnp.transpose(request, (1, 0))[0:1, :]
    to_slot = where01(iota((masters, buckets), 0).astype(F32) == at_slot).astype(BF16)
    receive(force_send, force_recv, 2)
    for f in range(FIELDS):
        arrived = force_recv[:, column(f)]
        for c in range(3):
            top, rest = halves(request[:, c + 1 : c + 2] * arrived)
            master_values[:, 3 * f + c, :] = dot16(to_slot, top, NN) + dot16(to_slot, rest, NN)
    total = add_rows(master_values, master_nodes, 0, masters // 8, node_tiles, total)
    for number in range(node_tiles):
        value = tile_sum(total, number)
        residual[:, column(number)] = value[0:3] - external_force[:, column(number)]
        jvp_one[:, column(number)] = value[3:6]
        jvp_two[:, column(number)] = value[6:9]

    sent(request_send, request_recv, 0)
    sent(master_send, master_recv, 1)
    sent(force_send, force_recv, 2)
    near_copy(halo_send, halo_recv, 0, before).wait_send()
    near_copy(ghost_send, ghost_recv, 1, after).wait_send()


def on_device(*arguments):
    arguments = list(arguments)
    displacement, slave_nodes, master_nodes = arguments[0], arguments[7], arguments[8]
    arguments[5] = arguments[5].reshape(1, -1)
    arguments[6] = arguments[6].reshape(1, -1)
    arguments[10] = arguments[10].reshape(1, -1)
    node_count = displacement.shape[1]
    slaves, masters = slave_nodes.shape[0], master_nodes.shape[0]
    corners = arguments[4].shape[0]
    layers = lax.axis_size("layer")
    devices = lax.axis_size("mesh") * layers
    capacity = max(2, 2 * slaves // devices)
    share = -(-capacity // 8) * 8
    buckets = devices * share
    vmem = lambda *shape: pltpu.VMEM(shape, F32)
    near = vmem(ROWS, LANES)
    wide = vmem(buckets, FIELDS * LANES)
    narrow = vmem(buckets, LANES)
    result = jax.ShapeDtypeStruct((3, node_count), F32)
    return pl.pallas_call(
        functools.partial(kernel, devices, layers, share),
        out_shape=(result, result, result),
        in_specs=[pl.BlockSpec(memory_space=pltpu.VMEM)] * len(arguments),
        out_specs=tuple([pl.BlockSpec(memory_space=pltpu.VMEM)] * 3),
        scratch_shapes=[
            vmem(ROWS, node_count + LANES),
            near,
            near,
            near,
            near,
            narrow,
            narrow,
            wide,
            wide,
            wide,
            wide,
            vmem(slaves, ROWS, LANES),
            vmem(corners, ROWS, LANES),
            vmem(masters, ROWS, LANES),
            pltpu.SemaphoreType.DMA((3, devices)),
            pltpu.SemaphoreType.DMA((3, devices)),
            pltpu.SemaphoreType.DMA((2,)),
            pltpu.SemaphoreType.DMA((2,)),
        ],
        compiler_params=pltpu.CompilerParams(
            collective_id=0, has_side_effects=True, vmem_limit_bytes=40 * 1024 * 1024
        ),
    )(*arguments)


def solution(mesh):
    split = ("groups", "mesh", "layer")
    wide, flat, tall = P(None, split), P(split), P(split, None)
    return jax.shard_map(
        on_device,
        mesh=mesh,
        in_specs=(wide,) * 5 + (flat, flat) + (tall,) * 3 + (flat,) + (tall,) * 3 + (P(), P()),
        out_specs=(wide, wide, wide),
        check_vma=False,
    )
```

time: 859 us -> 37.7 us (0.04)
  the two profiles are of different devices: /device:TPU:1 before, /device:TPU:0 now
where the time goes in v1:
time: 37.7 us; the launch traced here: 37 us
  Pallas kernels  25.9 us (69%)
  local copies, waits for them, and re-layouts  10.5 us (28%)
  between operations  0.7 us (2%)
    pallas_call x1, Pallas kernels, on_device(): pl.pallas_call(functools.partial(kernel, devices, layers, share), out_sha...  25.9 us
    unnamed x32, local copies, waits for them, and re-layouts  10.5 us

profile of v1, /device:TPU:0, one launch (start us, length us, event | category | flops | bytes accessed | tf_op | source)
XLA Modules:
  0.0 37.0 jit_solution(9317663610062709400)
XLA Ops:
  0.6 0.0 copy-start
  0.6 0.8 %copy.21.strain_operator = f32[48,24]{1,0:T(8,128)S(1)} copy(f32[48,24]{0,1:T(8,128)} %param.30) | data formatting | bytes 9216 | tf_op args[14]
  1.5 0.0 copy-start.1
  1.5 0.8 %copy.19.pair_owner = s32[64,1]{1,0:T(8,128)S(1)} copy(s32[64,1]{0,1:T(1,128)} %param.25) | data formatting | bytes 512 | tf_op args[9]
  2.2 0.0 copy-start.9
  2.2 0.8 %copy.20.normals = f32[64,3]{1,0:T(8,128)S(1)} copy(f32[64,3]{0,1:T(4,128)} %param.28) | data formatting | bytes 1536 | tf_op args[12]
  3.0 0.0 copy-done
  3.0 0.0 copy-done.1
  3.0 0.0 copy-done.5
  3.0 0.0 copy-done.9
  3.0 0.0 copy-start.2
  3.1 0.7 %copy-done.2 = s32[64,128]{1,0:T(8,128)S(1)} copy-done((s32[64,128]{1,0:T(8,128)S(1)}, s32[64,128]{1,0:T(8,128)}, u32[]{:S(2)}) %copy-start.2) | copy-done | bytes 32792
  3.8 0.8 %copy-done.3 = s32[64,128]{1,0:T(8,128)S(1)} copy-done((s32[64,128]{1,0:T(8,128)S(1)}, s32[64,128]{1,0:T(8,128)}, u32[]{:S(2)}) %copy-start.3) | copy-done | bytes 32792
  4.6 0.8 %copy-done.4 = f32[64,128]{1,0:T(8,128)S(1)} copy-done((f32[64,128]{1,0:T(8,128)S(1)}, f32[64,128]{1,0:T(8,128)}, u32[]{:S(2)}) %copy-start.4) | copy-done | bytes 32792
  5.3 0.7 %copy-done.6 = f32[3,512]{1,0:T(4,128)S(1)} copy-done((f32[3,512]{1,0:T(4,128)S(1)}, f32[3,512]{1,0:T(4,128)}, u32[]{:S(2)}) %copy-start.6) | copy-done | bytes 6168
  6.0 0.7 %copy-done.7 = f32[3,512]{1,0:T(4,128)S(1)} copy-done((f32[3,512]{1,0:T(4,128)S(1)}, f32[3,512]{1,0:T(4,128)}, u32[]{:S(2)}) %copy-start.7) | copy-done | bytes 6168
  6.7 0.7 %copy-done.8 = f32[3,512]{1,0:T(4,128)S(1)} copy-done((f32[3,512]{1,0:T(4,128)S(1)}, f32[3,512]{1,0:T(4,128)}, u32[]{:S(2)}) %copy-start.8) | copy-done | bytes 6168
  7.4 0.7 %copy-done.10 = f32[128]{0:T(128)S(1)} copy-done((f32[128]{0:T(128)S(1)}, f32[128]{0:T(128)}, u32[]{:S(2)}) %copy-start.10) | copy-done | bytes 536
  8.1 0.7 %copy-done.11 = s32[32]{0:T(128)S(1)} copy-done((s32[32]{0:T(128)S(1)}, s32[32]{0:T(128)}, u32[]{:S(2)}) %copy-start.11) | copy-done | bytes 152
  8.7 0.7 %copy-done.12 = s32[64]{0:T(128)S(1)} copy-done((s32[64]{0:T(128)S(1)}, s32[64]{0:T(128)}, u32[]{:S(2)}) %copy-start.12) | copy-done | bytes 280
  9.4 25.9 %shard_map.175 = (f32[3,512]{1,0:T(4,128)S(1)}, f32[3,512]{1,0:T(4,128)S(1)}, f32[3,512]{1,0:T(4,128)S(1)}) custom-call(f32[3,512]{1,0:T(4,128)S(1)} %copy-done.5, f32[3,512]{1,0:T(4,128)S(1)} %copy-done.6, f32[3,512]{1,0:T(4,128)S(1)} %copy-done.7, f32[3,512]{1,0:T(4,128)S(1)} %copy-done.8, s32[8,128]{1,0:T(8,128)S(1)} %copy-done.9, f32[1,128]{1,0:T(1,128)S(1)} %bitcast.3, ...), custom_call_target="tpu_custom_call" | custom-call | tf_op jit(solution)/shard_map/pallas_call | solution.py:408
  35.2 0.6 %copy.25 = f32[3,512]{1,0:T(4,128)} copy(f32[3,512]{1,0:T(4,128)S(1)} %get-tuple-element.6) | data formatting | bytes 12288
  35.8 0.6 %copy.26 = f32[3,512]{1,0:T(4,128)} copy(f32[3,512]{1,0:T(4,128)S(1)} %get-tuple-element.7) | data formatting | bytes 12288
  36.4 0.6 %copy.27 = f32[3,512]{1,0:T(4,128)} copy(f32[3,512]{1,0:T(4,128)S(1)} %get-tuple-element.8) | data formatting | bytes 12288
  (9 shorter events, 0.0 us)
Async XLA Ops:
  0.6 2.4 %copy-start = (f32[128,128]{1,0:T(8,128)S(1)}, f32[128,128]{1,0:T(8,128)}, u32[]{:S(2)}) copy-start(f32[128,128]{1,0:T(8,128)} %mortar.1) | copy-start | bytes 196612
  1.5 1.6 %copy-start.1 = (s32[64,128]{1,0:T(8,128)S(1)}, s32[64,128]{1,0:T(8,128)}, u32[]{:S(2)}) copy-start(s32[64,128]{1,0:T(8,128)} %slave_nodes.1) | copy-start | bytes 98308
  2.2 0.8 %copy-start.5 = (f32[3,512]{1,0:T(4,128)S(1)}, f32[3,512]{1,0:T(4,128)}, u32[]{:S(2)}) copy-start(f32[3,512]{1,0:T(4,128)} %displacement.1) | copy-start | bytes 18436
  2.2 0.8 %copy-start.9 = (s32[8,128]{1,0:T(8,128)S(1)}, s32[8,128]{1,0:T(8,128)}, u32[]{:S(2)}) copy-start(s32[8,128]{1,0:T(8,128)} %connectivity.1) | copy-start | bytes 12292
  3.0 0.8 %copy-start.2 = (s32[64,128]{1,0:T(8,128)S(1)}, s32[64,128]{1,0:T(8,128)}, u32[]{:S(2)}) copy-start(s32[64,128]{1,0:T(8,128)} %master_nodes.1) | copy-start | bytes 98308
  3.8 0.8 %copy-start.3 = (s32[64,128]{1,0:T(8,128)S(1)}, s32[64,128]{1,0:T(8,128)}, u32[]{:S(2)}) copy-start(s32[64,128]{1,0:T(8,128)} %active_flags.1) | copy-start | bytes 98308
  4.6 0.8 %copy-start.4 = (f32[64,128]{1,0:T(8,128)S(1)}, f32[64,128]{1,0:T(8,128)}, u32[]{:S(2)}) copy-start(f32[64,128]{1,0:T(8,128)} %initial_gap.1) | copy-start | bytes 98308
  5.3 0.7 %copy-start.6 = (f32[3,512]{1,0:T(4,128)S(1)}, f32[3,512]{1,0:T(4,128)}, u32[]{:S(2)}) copy-start(f32[3,512]{1,0:T(4,128)} %tangent_one.1) | copy-start | bytes 18436
  6.0 0.7 %copy-start.7 = (f32[3,512]{1,0:T(4,128)S(1)}, f32[3,512]{1,0:T(4,128)}, u32[]{:S(2)}) copy-start(f32[3,512]{1,0:T(4,128)} %tangent_two.1) | copy-start | bytes 18436
  6.7 0.7 %copy-start.8 = (f32[3,512]{1,0:T(4,128)S(1)}, f32[3,512]{1,0:T(4,128)}, u32[]{:S(2)}) copy-start(f32[3,512]{1,0:T(4,128)} %external_force.1) | copy-start | bytes 18436
  7.4 0.7 %copy-start.10 = (f32[128]{0:T(128)S(1)}, f32[128]{0:T(128)}, u32[]{:S(2)}) copy-start(f32[128]{0:T(128)} %param.21) | copy-start | bytes 1540
  8.1 0.7 %copy-start.11 = (s32[32]{0:T(128)S(1)}, s32[32]{0:T(128)}, u32[]{:S(2)}) copy-start(s32[32]{0:T(128)} %param.22) | copy-start | bytes 388
  8.7 0.7 %copy-start.12 = (s32[64]{0:T(128)S(1)}, s32[64]{0:T(128)}, u32[]{:S(2)}) copy-start(s32[64]{0:T(128)} %param.26) | copy-start | bytes 772

commit v2 on v1

--- a/solution.py
+++ b/solution.py
@@ -15,6 +15,7 @@
 NN = ((1,), (0,))
 NT = ((1,), (1,))
 TN = ((0,), (0,))
+LOAD_ORDER = (9, 10, 12, 0, 1, 2, 6, 8, 7, 4, 5, 14, 11, 13, 15, 3)
 F32 = jnp.float32
 BF16 = jnp.bfloat16
 
@@ -99,44 +100,49 @@
     devices,
     layers,
     share,
-    displacement,
-    tangent_one,
-    tangent_two,
-    external_force,
-    connectivity,
-    element_scale,
-    halo_nodes,
-    slave_nodes,
-    master_nodes,
-    pair_owner,
-    pair_slot,
-    active_flags,
-    normals,
-    initial_gap,
-    strain_operator,
-    mortar,
-    residual,
-    jvp_one,
-    jvp_two,
-    field,
-    halo_send,
-    halo_recv,
-    ghost_send,
-    ghost_recv,
-    request_send,
-    request_recv,
-    master_send,
-    master_recv,
-    force_send,
-    force_recv,
-    slave_values,
-    element_values,
-    master_values,
-    send_sem,
-    recv_sem,
-    near_send_sem,
-    near_recv_sem,
+    *refs,
 ):
+    sources, outputs, held, scratch = refs[:16], refs[16:19], refs[19:35], refs[35:]
+    (
+        displacement,
+        tangent_one,
+        tangent_two,
+        external_force,
+        connectivity,
+        element_scale,
+        halo_nodes,
+        slave_nodes,
+        master_nodes,
+        pair_owner,
+        pair_slot,
+        active_flags,
+        normals,
+        initial_gap,
+        strain_operator,
+        mortar,
+    ) = held
+    residual, jvp_one, jvp_two = outputs
+    (
+        field,
+        halo_send,
+        halo_recv,
+        ghost_send,
+        ghost_recv,
+        request_send,
+        request_recv,
+        master_send,
+        master_recv,
+        force_send,
+        force_recv,
+        slave_values,
+        element_values,
+        master_values,
+        send_sem,
+        recv_sem,
+        near_send_sem,
+        near_recv_sem,
+        input_sem,
+    ) = scratch
     node_count = displacement.shape[1]
     node_tiles = node_count // LANES
     slaves = slave_nodes.shape[0]
@@ -198,6 +204,17 @@
     after = lax.rem(me + 1, devices)
     before = lax.rem(me + devices - 1, devices)
 
+    loads = [
+        pltpu.make_async_copy(source, target, input_sem.at[number])
+        for number, source, target in zip(range(len(sources)), sources, held)
+    ]
+    for number in LOAD_ORDER:
+        loads[number].start()
+
+    def ready(*numbers):
+        for number in numbers:
+            loads[number].wait()
+
     barrier = pltpu.get_barrier_semaphore()
 
     def greet(k, carry):
@@ -211,27 +228,31 @@
 
     lax.fori_loop(1, devices, greet, 0)
 
-    owner_column = pair_owner[...].astype(F32)
+    ready(9, 10, 12)
     first = iota((slaves, slaves), 0)
     second = iota((slaves, slaves), 1)
-    owner_row = jnp.sum(jnp.where(first == second, owner_column, 0.0), axis=0, keepdims=True)
-    slot_column = jnp.sum(
-        jnp.where(first == second, pair_slot[...].astype(F32), 0.0), axis=1, keepdims=True
-    )
+
+    def stand(row):
+        return jnp.sum(jnp.where(first == second, row, 0.0), axis=1, keepdims=True)
+
+    owner_row = pair_owner[...].astype(F32)
+    owner_column = stand(owner_row)
+    slot_column = stand(pair_slot[...].astype(F32))
+    normal = [stand(normals[c : c + 1, :]) for c in range(3)]
     same = where01(owner_column == owner_row)
     rank_row = jnp.sum(jnp.where(first < second, same, 0.0), axis=0, keepdims=True)
     rank_column = jnp.sum(jnp.where(second < first, same, 0.0), axis=1, keepdims=True)
     bucket_row = owner_row * share + rank_row
     bucket_column = owner_column * share + rank_column
     to_bucket = where01(iota((buckets, slaves), 0).astype(F32) == bucket_row)
-    normal = normals[...]
     lane = iota((slaves, LANES), 1)
     wanted = jnp.where(lane == 0, slot_column, 0.0)
     for c in range(3):
-        wanted = jnp.where(lane == c + 1, normal[:, c : c + 1], wanted)
+        wanted = jnp.where(lane == c + 1, normal[c], wanted)
     request_send[...] = dot(to_bucket, wanted, NN)
 
     field[...] = jnp.zeros(field.shape, F32)
+    ready(0, 1, 2, 6)
     for f, source in enumerate((displacement, tangent_one, tangent_two)):
         field[3 * f : 3 * f + 3, 0:node_count] = source[...]
     ghosts = halo_nodes.shape[1]
@@ -251,6 +272,7 @@
     def nodal(index, fc):
         return lookup(lambda number: field[fc : fc + 1, column(number)], node_tiles, index)
 
+    ready(8)
     master_index = master_nodes[...]
     parts = [thirds(nodal(master_index, fc)) for fc in range(9)]
     served = jnp.concatenate(
@@ -270,16 +292,19 @@
         master_send[:, column(f)] = value
     send(master_send, master_recv, 1)
 
+    ready(7)
     slave_index = slave_nodes[...]
     slave_normal = []
     for f in range(FIELDS):
-        value = normal[:, 0:1] * nodal(slave_index, 3 * f)
+        value = normal[0] * nodal(slave_index, 3 * f)
         for c in range(1, 3):
-            value = value + normal[:, c : c + 1] * nodal(slave_index, 3 * f + c)
+            value = value + normal[c] * nodal(slave_index, 3 * f + c)
         slave_normal.append(value)
     live = jnp.where(slave_index < node_count, PENALTY, 0.0)
+    ready(11)
     weight = active_flags[...].astype(F32) * live
 
+    ready(4, 5, 14)
     near_copy(halo_send, halo_recv, 0, before).wait_recv()
     field[:, node_count : node_count + LANES] = halo_recv[...]
     corner = connectivity[...]
@@ -300,14 +325,14 @@
         ],
         axis=1,
     )
-    entries = strain_operator.shape[1]
-    order = iota((entries, entries), 1)
+    entries = strain_operator.shape[0]
+    order = iota((entries, entries), 0)
     operator = dot(
+        where01(iota((entries, entries), 1) == 3 * lax.rem(order, 8) + order // 8),
         strain_operator[...],
-        where01(iota((entries, entries), 0) == 3 * lax.rem(order, 8) + order // 8),
         NN,
     )
-    strain = dot(operator, elements, NN)
+    strain = dot(operator, elements, TN)
     scale = element_scale[...]
     base = strain[:, 0:LANES]
     hyperbolic = jnp.tanh(base)
@@ -320,7 +345,7 @@
         ],
         axis=1,
     )
-    element_force = dot(operator, stress, TN)
+    element_force = dot(operator, stress, NN)
     element_values[...] = jnp.zeros(element_values.shape, F32)
     for f in range(FIELDS):
         for c in range(3):
@@ -331,6 +356,7 @@
     near_copy(ghost_send, ghost_recv, 1, after).start()
     total = total[: 2 * ROWS * node_tiles]
 
+    ready(13, 15, 3)
     receive(master_send, master_recv, 1)
     from_bucket = where01(iota((slaves, buckets), 1).astype(F32) == bucket_column).astype(BF16)
     top, rest = halves(master_recv[...])
@@ -356,7 +382,7 @@
     slave_values[...] = jnp.zeros(slave_values.shape, F32)
     for f in range(FIELDS):
         for c in range(3):
-            slave_values[:, 3 * f + c, :] = -normal[:, c : c + 1] * multiplier[f]
+            slave_values[:, 3 * f + c, :] = -normal[c] * multiplier[f]
     total = add_rows(slave_values, slave_nodes, 0, slaves // 8, node_tiles, total)
 
     near_copy(ghost_send, ghost_recv, 1, after).wait_recv()
@@ -391,7 +417,10 @@
     displacement, slave_nodes, master_nodes = arguments[0], arguments[7], arguments[8]
     arguments[5] = arguments[5].reshape(1, -1)
     arguments[6] = arguments[6].reshape(1, -1)
+    arguments[9] = arguments[9].T
     arguments[10] = arguments[10].reshape(1, -1)
+    arguments[12] = arguments[12].T
+    arguments[14] = arguments[14].T
     node_count = displacement.shape[1]
     slaves, masters = slave_nodes.shape[0], master_nodes.shape[0]
     corners = arguments[4].shape[0]
@@ -408,9 +437,10 @@
     return pl.pallas_call(
         functools.partial(kernel, devices, layers, share),
         out_shape=(result, result, result),
-        in_specs=[pl.BlockSpec(memory_space=pltpu.VMEM)] * len(arguments),
+        in_specs=[pl.BlockSpec(memory_space=pltpu.HBM)] * len(arguments),
         out_specs=tuple([pl.BlockSpec(memory_space=pltpu.VMEM)] * 3),
-        scratch_shapes=[
+        scratch_shapes=[pltpu.VMEM(each.shape, each.dtype) for each in arguments]
+        + [
             vmem(ROWS, node_count + LANES),
             near,
             near,
@@ -429,9 +459,10 @@
             pltpu.SemaphoreType.DMA((3, devices)),
             pltpu.SemaphoreType.DMA((2,)),
             pltpu.SemaphoreType.DMA((2,)),
+            pltpu.SemaphoreType.DMA((len(arguments),)),
         ],
         compiler_params=pltpu.CompilerParams(
-            collective_id=0, has_side_effects=True, vmem_limit_bytes=40 * 1024 * 1024
+            collective_id=0, has_side_effects=True, vmem_limit_bytes=63 * 1024 * 1024
         ),
     )(*arguments)
 

time: 37.7 us -> 30.3 us (0.80)
  local copies, waits for them, and re-layouts: 10.5 us -> 2.61 us
  Pallas kernels: 25.9 us -> 26.7 us
    unnamed x32 -> x7, local copies, waits for them, and re-layouts: 10.5 us -> 2.61 us
    pallas_call x1, Pallas kernels: 25.9 us -> 26.7 us  [on_device(): pl.pallas_call(functools.partial(kernel, devices, layers, share), out_sha...]
where the time goes in v2:
time: 30.3 us; the launch traced here: 30 us
  Pallas kernels  26.7 us (88%)
  local copies, waits for them, and re-layouts  2.61 us (9%)
  between operations  0.66 us (2%)
    pallas_call x1, Pallas kernels, on_device(): pl.pallas_call(functools.partial(kernel, devices, layers, share), out_sha...  26.7 us
    unnamed x7, local copies, waits for them, and re-layouts  2.61 us

profile of v2, /device:TPU:0, one launch (start us, length us, event | category | flops | bytes accessed | tf_op | source)
XLA Modules:
  0.0 30.0 jit_solution(4435263976575108942)
XLA Ops:
  0.6 26.7 %shard_map.175 = (f32[3,512]{1,0:T(4,128)}, f32[3,512]{1,0:T(4,128)}, f32[3,512]{1,0:T(4,128)}) custom-call(f32[3,512]{1,0:T(4,128)} %refs_0_.1, f32[3,512]{1,0:T(4,128)} %refs_1_.1, f32[3,512]{1,0:T(4,128)} %refs_2_.1, f32[3,512]{1,0:T(4,128)} %refs_3_.1, s32[8,128]{1,0:T(8,128)} %refs_4_.1, f32[1,128]{1,0:T(1,128)} %bitcast.8, s32[1,32]{1,0:T(1,128)} %bitcast.9, ...), custom_call_target="tpu_custom_call" | custom-call | tf_op jit(solution)/shard_map/pallas_call | solution.py:437
  27.4 0.0 copy-start.1
  27.4 1.3 %copy.22 = f32[3,512]{1,0:T(4,128)} copy(f32[3,512]{1,0:T(4,128)} %get-tuple-element.6) | data formatting | bytes 12288
  28.7 0.0 copy-done.1
  28.7 0.0 copy-start
  28.7 0.6 %copy.23 = f32[3,512]{1,0:T(4,128)} copy(f32[3,512]{1,0:T(4,128)S(1)} %copy-done.1) | data formatting | bytes 12288
  29.3 0.1 copy-done
  29.4 0.6 %copy.24 = f32[3,512]{1,0:T(4,128)} copy(f32[3,512]{1,0:T(4,128)S(1)} %copy-done) | data formatting | bytes 12288
Async XLA Ops:
  27.4 1.3 %copy-start.1 = (f32[3,512]{1,0:T(4,128)S(1)}, f32[3,512]{1,0:T(4,128)}, u32[]{:S(2)}) copy-start(f32[3,512]{1,0:T(4,128)} %get-tuple-element.7) | copy-start | bytes 18436
  28.7 0.7 %copy-start = (f32[3,512]{1,0:T(4,128)S(1)}, f32[3,512]{1,0:T(4,128)}, u32[]{:S(2)}) copy-start(f32[3,512]{1,0:T(4,128)} %get-tuple-element.8) | copy-start | bytes 18436

commit v3 on v2

v3 whole, which is shorter than its diff:
```python
import functools

import jax
import jax.numpy as jnp
from jax import lax
from jax.experimental import pallas as pl
from jax.experimental.pallas import tpu as pltpu
from jax.sharding import PartitionSpec as P

PENALTY = 2.0
HIGH = lax.Precision.HIGHEST
LANES = 128
ROWS = 16
FIELDS = 3
PHASES = 1 + 2 * FIELDS
NN = ((1,), (0,))
NT = ((1,), (1,))
TN = ((0,), (0,))
LOAD_ORDER = (9, 10, 12, 0, 1, 2, 6, 8, 7, 4, 5, 14, 11, 13, 15, 3)
F32 = jnp.float32
BF16 = jnp.bfloat16


def dot(left, right, dims):
    return lax.dot_general(
        left, right, (dims, ((), ())), precision=HIGH, preferred_element_type=F32
    )


def dot16(left, right, dims):
    return lax.dot_general(left, right, (dims, ((), ())), preferred_element_type=F32)


def halves(value):
    top = value.astype(BF16)
    return top, (value - top.astype(F32)).astype(BF16)


def thirds(value):
    top = value.astype(BF16)
    rest = value - top.astype(F32)
    middle = rest.astype(BF16)
    return top, middle, (rest - middle.astype(F32)).astype(BF16)


def iota(shape, dim):
    return lax.broadcasted_iota(jnp.int32, shape, dim)


def where01(mask):
    return jnp.where(mask, 1.0, 0.0).astype(F32)


def column(index, by=LANES):
    return slice(index * by, (index + 1) * by)


def lookup(tile_of, tiles, index):
    lane = jnp.bitwise_and(index, LANES - 1)
    tile = jnp.right_shift(index, 7)
    found = jnp.zeros(index.shape, F32)
    for number in range(tiles):
        table = jnp.broadcast_to(tile_of(number), index.shape)
        picked = jnp.take_along_axis(table, lane, axis=1, mode="promise_in_bounds")
        found = jnp.where(tile == number, picked, found)
    return found


def left_operand(values, index, tiles):
    tile = jnp.right_shift(index, 7)
    top = values.astype(BF16).astype(F32)
    both = jnp.concatenate([top, values - top], axis=0)
    return jnp.concatenate(
        [jnp.where(tile == number, both, 0.0).astype(BF16) for number in range(tiles)], axis=0
    )


def right_operand(index):
    lane = jnp.bitwise_and(index, LANES - 1)
    return where01(lane == iota((LANES, LANES), 0)).astype(BF16)


def eight_rows(index_ref, group):
    return index_ref[pl.ds(pl.multiple_of(group * 8, 8), 8), :]


def fill_right(right_ref, index_ref, groups):
    def step(group, carry):
        rows = eight_rows(index_ref, group)
        for k in range(8):
            right_ref[group, :, column(k)] = right_operand(rows[k : k + 1, :])
        return carry

    lax.fori_loop(0, groups, step, 0)


def add_rows(value_ref, index_ref, right_ref, groups, tiles, total):
    def step(group, total):
        rows = eight_rows(index_ref, group)
        left = [left_operand(value_ref[group * 8 + k], rows[k : k + 1, :], tiles) for k in range(8)]
        return total + dot16(jnp.concatenate(left, axis=1), right_ref[group], NT)

    return lax.fori_loop(0, groups, step, total)


def three_products(value, factor, dims):
    top, rest = halves(value)
    return dot16(jnp.concatenate([top, top, rest], axis=1), factor, dims)


def tile_sum(total, number):
    start = number * 2 * ROWS
    return total[start : start + ROWS] + total[start + ROWS : start + 2 * ROWS]


def kernel(
    devices,
    layers,
    share,
    *refs,
):
    sources, outputs, held, scratch = refs[:16], refs[16:17], refs[17:33], refs[33:]
    (
        displacement,
        tangent_one,
        tangent_two,
        external_force,
        connectivity,
        element_scale,
        halo_nodes,
        slave_nodes,
        master_nodes,
        pair_owner,
        pair_slot,
        active_flags,
        normals,
        initial_gap,
        strain_operator,
        mortar,
    ) = held
    (result,) = outputs
    (
        field,
        halo_send,
        halo_recv,
        ghost_send,
        ghost_recv,
        outbox,
        inbox,
        slave_values,
        element_values,
        master_values,
        slave_right,
        element_right,
        master_right,
        send_sem,
        recv_sem,
        near_send_sem,
        near_recv_sem,
        input_sem,
    ) = scratch
    node_count = displacement.shape[1]
    node_tiles = node_count // LANES
    slaves = slave_nodes.shape[0]
    masters = master_nodes.shape[0]
    buckets = devices * share
    group = lax.axis_index("groups")
    me = lax.axis_index("mesh") * layers + lax.axis_index("layer")

    after = lax.rem(me + 1, devices)
    before = lax.rem(me + devices - 1, devices)

    def device(peer):
        return (group, peer // layers, lax.rem(peer, layers))

    def block(ref, phase, peer):
        return ref.at[phase, pl.ds(pl.multiple_of(peer * share, share), share), :]

    def send(phase):
        def one(k, carry):
            peer = lax.rem(me + k, devices)
            pltpu.make_async_remote_copy(
                src_ref=block(outbox, phase, peer),
                dst_ref=block(inbox, phase, me),
                send_sem=send_sem.at[phase],
                recv_sem=recv_sem.at[phase],
                device_id=device(peer),
                device_id_type=pl.DeviceIdType.MESH,
            ).start()
            return carry

        lax.fori_loop(1, devices, one, 0)
        mine = pl.ds(pl.multiple_of(me * share, share), share)
        inbox[phase, mine, :] = outbox[phase, mine, :]

    def whole(phase):
        rows = pl.ds(0, buckets - share)
        return pltpu.make_async_remote_copy(
            src_ref=outbox.at[phase, rows, :],
            dst_ref=inbox.at[phase, rows, :],
            send_sem=send_sem.at[phase],
            recv_sem=recv_sem.at[phase],
            device_id=device(after),
            device_id_type=pl.DeviceIdType.MESH,
        )

    def receive(phase):
        whole(phase).wait_recv()

    def sent(phase):
        whole(phase).wait_send()

    def near_copy(source, target, number, peer):
        return pltpu.make_async_remote_copy(
            src_ref=source,
            dst_ref=target,
            send_sem=near_send_sem.at[number],
            recv_sem=near_recv_sem.at[number],
            device_id=device(peer),
            device_id_type=pl.DeviceIdType.MESH,
        )

    barrier = pltpu.get_barrier_semaphore()

    def greet(k, carry):
        pl.semaphore_signal(
            barrier,
            inc=1,
            device_id=device(lax.rem(me + k, devices)),
            device_id_type=pl.DeviceIdType.MESH,
        )
        return carry

    lax.fori_loop(1, devices, greet, 0)

    loads = [
        pltpu.make_async_copy(source, target, input_sem.at[number])
        for number, source, target in zip(range(len(sources)), sources, held)
    ]
    for number in LOAD_ORDER:
        loads[number].start()

    def ready(*numbers):
        for number in numbers:
            loads[number].wait()

    ready(9, 10, 12)
    first = iota((slaves, slaves), 0)
    second = iota((slaves, slaves), 1)

    def stand(row):
        return jnp.sum(jnp.where(first == second, row, 0.0), axis=1, keepdims=True)

    owner_row = pair_owner[...].astype(F32)
    owner_column = stand(owner_row)
    slot_column = stand(pair_slot[...].astype(F32))
    normal = [stand(normals[c : c + 1, :]) for c in range(3)]
    same = where01(owner_column == owner_row)
    rank_row = jnp.sum(jnp.where(first < second, same, 0.0), axis=0, keepdims=True)
    rank_column = jnp.sum(jnp.where(second < first, same, 0.0), axis=1, keepdims=True)
    bucket_row = owner_row * share + rank_row
    bucket_column = owner_column * share + rank_column
    to_bucket = where01(iota((buckets, slaves), 0).astype(F32) == bucket_row)
    lane = iota((slaves, LANES), 1)
    wanted = jnp.where(lane == 0, slot_column, 0.0)
    for c in range(3):
        wanted = jnp.where(lane == c + 1, normal[c], wanted)
    outbox[0] = dot(to_bucket, wanted, NN)

    field[...] = jnp.zeros(field.shape, F32)
    ready(0, 1, 2, 6)
    for f, source in enumerate((displacement, tangent_one, tangent_two)):
        field[3 * f : 3 * f + 3, 0:node_count] = source[...]
    ghosts = halo_nodes.shape[1]
    halo_row = jnp.concatenate(
        [halo_nodes[...], jnp.full((1, LANES - ghosts), node_count, jnp.int32)], axis=1
    )
    halo_send[...] = lookup(
        lambda number: field[:, column(number)],
        node_tiles,
        jnp.broadcast_to(halo_row, (ROWS, LANES)),
    )


    def nodal(index, fc):
        return lookup(lambda number: field[fc : fc + 1, column(number)], node_tiles, index)

    ready(8)
    master_index = master_nodes[...]
    parts = [thirds(nodal(master_index, fc)) for fc in range(9)]
    served = jnp.concatenate(
        [jnp.concatenate([part[k] for part in parts], axis=1) for k in range(3)], axis=0
    )
    ready(7)
    slave_index = slave_nodes[...]
    slave_normal = []
    for f in range(FIELDS):
        value = normal[0] * nodal(slave_index, 3 * f)
        for c in range(1, 3):
            value = value + normal[c] * nodal(slave_index, 3 * f + c)
        slave_normal.append(value)

    pl.semaphore_wait(barrier, devices - 1)
    send(0)
    near_copy(halo_send, halo_recv, 0, before).start()

    ready(4, 5, 11, 13, 14, 15, 3)
    live = jnp.where(slave_index < node_count, PENALTY, 0.0)
    weight = active_flags[...].astype(F32) * live
    top, rest = halves(mortar[...])
    mortar_rows = jnp.concatenate([top, rest, top], axis=0)
    mortar_columns = jnp.concatenate([top, rest, top], axis=1)
    fill_right(slave_right, slave_nodes, slaves // 8)
    fill_right(element_right, connectivity, 1)
    fill_right(master_right, master_nodes, masters // 8)

    receive(0)
    request = inbox[0]
    pick = where01(
        lax.rem(iota((buckets, 3 * masters), 1), masters).astype(F32) == request[:, 0:1]
    ).astype(BF16)
    for f in range(FIELDS):
        chosen = dot16(pick, served[:, column(f, 3 * LANES)], NN)
        value = request[:, 1:2] * chosen[:, column(0)]
        for c in range(1, 3):
            value = value + request[:, c + 1 : c + 2] * chosen[:, column(c)]
        outbox[1 + f] = value
        send(1 + f)

    near_copy(halo_send, halo_recv, 0, before).wait_recv()
    field[:, node_count : node_count + LANES] = halo_recv[...]
    corner = connectivity[...]
    elements = jnp.concatenate(
        [
            jnp.concatenate(
                [
                    lookup(
                        lambda number: field[3 * f + c : 3 * f + c + 1, column(number)],
                        node_tiles + 1,
                        corner,
                    )
                    for c in range(3)
                ],
                axis=0,
            )
            for f in range(FIELDS)
        ],
        axis=1,
    )
    entries = strain_operator.shape[0]
    order = iota((entries, entries), 0)
    operator = dot(
        where01(iota((entries, entries), 1) == 3 * lax.rem(order, 8) + order // 8),
        strain_operator[...],
        NN,
    )
    strain = dot(operator, elements, TN)
    scale = element_scale[...]
    base = strain[:, 0:LANES]
    hyperbolic = jnp.tanh(base)
    stiffness = scale * (1.0 + 0.5 * (1.0 - hyperbolic * hyperbolic))
    stress = jnp.concatenate(
        [
            scale * (base + 0.5 * hyperbolic),
            stiffness * strain[:, column(1)],
            stiffness * strain[:, column(2)],
        ],
        axis=1,
    )
    element_force = dot(operator, stress, NN)
    element_values[...] = jnp.zeros(element_values.shape, F32)
    for f in range(FIELDS):
        for c in range(3):
            element_values[:, 3 * f + c, :] = element_force[8 * c : 8 * c + 8, column(f)]
    total = jnp.zeros((2 * ROWS * (node_tiles + 1), LANES), F32)
    total = add_rows(element_values, connectivity, element_right, 1, node_tiles + 1, total)
    ghost_send[...] = tile_sum(total, node_tiles)
    near_copy(ghost_send, ghost_recv, 1, after).start()
    total = total[: 2 * ROWS * node_tiles]

    from_bucket = where01(iota((slaves, buckets), 1).astype(F32) == bucket_column).astype(BF16)
    to_bucket = to_bucket.astype(BF16)
    multiplier = []
    slope = None
    for f in range(FIELDS):
        receive(1 + f)
        top, rest = halves(inbox[1 + f])
        fetched = dot16(from_bucket, top, NN) + dot16(from_bucket, rest, NN)
        change = slave_normal[f] - three_products(fetched, mortar_columns, NT)
        if f == 0:
            closing = -(initial_gap[...] + change)
            small = jnp.exp(-jnp.abs(closing))
            slope = -weight * jnp.where(closing >= 0.0, 1.0, small) / (1.0 + small)
            multiplier.append(weight * (jnp.maximum(closing, 0.0) + jnp.log1p(small)))
        else:
            multiplier.append(slope * change)
        top, rest = halves(three_products(multiplier[f], mortar_rows, NN))
        outbox[4 + f] = dot16(to_bucket, top, NN) + dot16(to_bucket, rest, NN)
        send(4 + f)

    slave_values[...] = jnp.zeros(slave_values.shape, F32)
    for f in range(FIELDS):
        for c in range(3):
            slave_values[:, 3 * f + c, :] = -normal[c] * multiplier[f]
    total = add_rows(slave_values, slave_nodes, slave_right, slaves // 8, node_tiles, total)

    near_copy(ghost_send, ghost_recv, 1, after).wait_recv()
    total = total + dot16(
        left_operand(ghost_recv[...], halo_row, node_tiles), right_operand(halo_row), NT
    )

    master_values[...] = jnp.zeros(master_values.shape, F32)
    at_slot = jnp.transpose(request, (1, 0))[0:1, :]
    to_slot = where01(iota((masters, buckets), 0).astype(F32) == at_slot).astype(BF16)
    for f in range(FIELDS):
        receive(4 + f)
        arrived = inbox[4 + f]
        for c in range(3):
            top, rest = halves(request[:, c + 1 : c + 2] * arrived)
            master_values[:, 3 * f + c, :] = dot16(to_slot, top, NN) + dot16(to_slot, rest, NN)
    total = add_rows(master_values, master_nodes, master_right, masters // 8, node_tiles, total)
    for number in range(node_tiles):
        value = tile_sum(total, number)
        result[0:3, column(number)] = value[0:3] - external_force[:, column(number)]
        result[3:9, column(number)] = value[3:9]

    for phase in range(PHASES):
        sent(phase)
    near_copy(halo_send, halo_recv, 0, before).wait_send()
    near_copy(ghost_send, ghost_recv, 1, after).wait_send()


def on_device(*arguments):
    arguments = list(arguments)
    displacement, slave_nodes, master_nodes = arguments[0], arguments[7], arguments[8]
    arguments[5] = arguments[5].reshape(1, -1)
    arguments[6] = arguments[6].reshape(1, -1)
    arguments[9] = arguments[9].T
    arguments[10] = arguments[10].reshape(1, -1)
    arguments[12] = arguments[12].T
    arguments[14] = arguments[14].T
    node_count = displacement.shape[1]
    slaves, masters = slave_nodes.shape[0], master_nodes.shape[0]
    corners = arguments[4].shape[0]
    layers = lax.axis_size("layer")
    devices = lax.axis_size("mesh") * layers
    capacity = max(2, 2 * slaves // devices)
    share = -(-capacity // 8) * 8
    buckets = devices * share
    vmem = lambda *shape: pltpu.VMEM(shape, F32)
    near = vmem(ROWS, LANES)
    mail = vmem(PHASES, buckets, LANES)
    rights = [pltpu.VMEM((rows // 8, LANES, 8 * LANES), BF16) for rows in (slaves, corners, masters)]
    result = jax.ShapeDtypeStruct((9, node_count), F32)
    result = pl.pallas_call(
        functools.partial(kernel, devices, layers, share),
        out_shape=result,
        in_specs=[pl.BlockSpec(memory_space=pltpu.HBM)] * len(arguments),
        out_specs=pl.BlockSpec(memory_space=pltpu.VMEM),
        scratch_shapes=[pltpu.VMEM(each.shape, each.dtype) for each in arguments]
        + [
            vmem(ROWS, node_count + LANES),
            near,
            near,
            near,
            near,
            mail,
            mail,
            vmem(slaves, ROWS, LANES),
            vmem(corners, ROWS, LANES),
            vmem(masters, ROWS, LANES),
            *rights,
            pltpu.SemaphoreType.DMA((PHASES,)),
            pltpu.SemaphoreType.DMA((PHASES,)),
            pltpu.SemaphoreType.DMA((2,)),
            pltpu.SemaphoreType.DMA((2,)),
            pltpu.SemaphoreType.DMA((len(arguments),)),
        ],
        compiler_params=pltpu.CompilerParams(
            collective_id=0, has_side_effects=True, vmem_limit_bytes=63 * 1024 * 1024
        ),
    )(*arguments)
    return result[0:3], result[3:6], result[6:9]


def solution(mesh):
    split = ("groups", "mesh", "layer")
    wide, flat, tall = P(None, split), P(split), P(split, None)
    return jax.shard_map(
        on_device,
        mesh=mesh,
        in_specs=(wide,) * 5 + (flat, flat) + (tall,) * 3 + (flat,) + (tall,) * 3 + (P(), P()),
        out_specs=(wide, wide, wide),
        check_vma=False,
    )
```

time: 30.3 us -> 28.7 us (0.947)
  local copies, waits for them, and re-layouts: 2.61 us -> 1.45 us
    unnamed x7 -> x0, local copies, waits for them, and re-layouts: 2.61 us -> none
    slice x0 -> x1, local copies, waits for them, and re-layouts: none -> 1.45 us  [on_device(): return (result[0:3], result[3:6], result[6:9])]
    pallas_call x1, Pallas kernels: 26.7 us -> 26.4 us  [on_device(): pl.pallas_call(functools.partial(kernel, devices, layers, share), out_sha...]
where the time goes in v3:
time: 28.7 us; the launch traced here: 28.5 us
  Pallas kernels  26.4 us (92%)
  local copies, waits for them, and re-layouts  1.45 us (5%)
  between operations  0.65 us (2%)
    pallas_call x1, Pallas kernels, on_device(): pl.pallas_call(functools.partial(kernel, devices, layers, share), out_sha...  26.4 us
    slice x1, local copies, waits for them, and re-layouts, on_device(): return (result[0:3], result[3:6], result[6:9])  1.45 us

profile of v3, /device:TPU:0, one launch (start us, length us, event | category | flops | bytes accessed | tf_op | source)
XLA Modules:
  0.0 28.5 jit_solution(7275149430372157603)
XLA Ops:
  0.6 26.4 %shard_map.175 = f32[9,512]{1,0:T(8,128)} custom-call(f32[3,512]{1,0:T(4,128)} %refs_0_.1, f32[3,512]{1,0:T(4,128)} %refs_1_.1, f32[3,512]{1,0:T(4,128)} %refs_2_.1, f32[3,512]{1,0:T(4,128)} %refs_3_.1, s32[8,128]{1,0:T(8,128)} %refs_4_.1, f32[1,128]{1,0:T(1,128)} %bitcast.8, s32[1,32]{1,0:T(1,128)} %bitcast.9, s32[64,128]{1,0:T(8,128)} %refs_7_.1, ...), custom_call_target="tpu_custom_call" | custom-call | tf_op jit(solution)/shard_map/pallas_call | solution.py:455
  27.0 1.4 %fusion = (f32[3,512]{1,0:T(4,128)}, f32[3,512]{1,0:T(4,128)}, f32[3,512]{1,0:T(4,128)}) fusion(f32[9,512]{1,0:T(8,128)} %shard_map.175), kind=kLoop, calls=%fused_computation | loop fusion | bytes 36864 | tf_op jit(solution)/shard_map/slice | solution.py:483

commit v4 on v3

--- a/solution.py
+++ b/solution.py
@@ -100,7 +100,7 @@
         left = [left_operand(value_ref[group * 8 + k], rows[k : k + 1, :], tiles) for k in range(8)]
         return total + dot16(jnp.concatenate(left, axis=1), right_ref[group], NT)
 
-    return lax.fori_loop(0, groups, step, total)
+    return lax.fori_loop(0, groups, step, total, unroll=2 if groups > 1 else 1)
 
 
 def three_products(value, factor, dims):
@@ -189,7 +189,7 @@
             ).start()
             return carry
 
-        lax.fori_loop(1, devices, one, 0)
+        lax.fori_loop(1, devices, one, 0, unroll=devices <= 16)
         mine = pl.ds(pl.multiple_of(me * share, share), share)
         inbox[phase, mine, :] = outbox[phase, mine, :]
 

time: 28.7 us -> 27.4 us (0.955)
  Pallas kernels: 26.4 us -> 25.1 us
    pallas_call x1, Pallas kernels: 26.4 us -> 25.1 us  [on_device(): pl.pallas_call(functools.partial(kernel, devices, layers, share), out_sha...]
where the time goes in v4:
time: 27.4 us; the launch traced here: 27.2 us
  Pallas kernels  25.1 us (92%)
  local copies, waits for them, and re-layouts  1.45 us (5%)
  between operations  0.65 us (2%)
    pallas_call x1, Pallas kernels, on_device(): pl.pallas_call(functools.partial(kernel, devices, layers, share), out_sha...  25.1 us
    slice x1, local copies, waits for them, and re-layouts, on_device(): return (result[0:3], result[3:6], result[6:9])  1.45 us

profile of v4, /device:TPU:0, one launch (start us, length us, event | category | flops | bytes accessed | tf_op | source)
XLA Modules:
  0.0 27.2 jit_solution(8323409732862275376)
XLA Ops:
  0.6 25.1 %shard_map.175 = f32[9,512]{1,0:T(8,128)} custom-call(f32[3,512]{1,0:T(4,128)} %refs_0_.1, f32[3,512]{1,0:T(4,128)} %refs_1_.1, f32[3,512]{1,0:T(4,128)} %refs_2_.1, f32[3,512]{1,0:T(4,128)} %refs_3_.1, s32[8,128]{1,0:T(8,128)} %refs_4_.1, f32[1,128]{1,0:T(1,128)} %bitcast.8, s32[1,32]{1,0:T(1,128)} %bitcast.9, s32[64,128]{1,0:T(8,128)} %refs_7_.1, ...), custom_call_target="tpu_custom_call" | custom-call | tf_op jit(solution)/shard_map/pallas_call | solution.py:455
  25.8 1.4 %fusion = (f32[3,512]{1,0:T(4,128)}, f32[3,512]{1,0:T(4,128)}, f32[3,512]{1,0:T(4,128)}) fusion(f32[9,512]{1,0:T(8,128)} %shard_map.175), kind=kLoop, calls=%fused_computation | loop fusion | bytes 36864 | tf_op jit(solution)/shard_map/slice | solution.py:483
